TPU v7x, 32 devices: a whole 2x2x4 slice. The times are simulated.
32 devices in a mesh: groups: 2 (over x), cells: 16 (over z, y, core).
Axes of the slice: x: 2, y: 2, z: 4, core: 2. Of those that a mesh axis runs over, the one named last changes fastest.
Arguments:
- features: bfloat16 [12288, 384], P(('groups', 'cells')), parts along dimension 0, may hold values from -40 to 40
- cotangent: bfloat16 [12288, 384], P(('groups', 'cells')), parts along dimension 0, may hold values from -6 to 6
- inner_weight: bfloat16 [384, 1152], replicated, may hold values from -0.3125 to 0.3125
- outer_weight: bfloat16 [384, 384], replicated, may hold values from -0.3125 to 0.3125
- upward_weight: bfloat16 [384, 1536], replicated, may hold values from -0.3125 to 0.3125
- downward_weight: bfloat16 [1536, 384], replicated, may hold values from -0.15625 to 0.15625
- node_mask: int32 [96, 128], P(('groups', 'cells')), parts along dimension 0, may hold values from 0 to 1, as said below
- neighbours: int32 [96, 8], P(('groups', 'cells')), parts along dimension 0, may hold values from 0 to 47, as said below
Outputs:
- back_features: bfloat16 [12288, 384], P(('groups', 'cells')), parts along dimension 0
- grad_inner: float32 [768, 1152], P(('groups', 'cells')), parts along dimension 0
- grad_outer: float32 [768, 384], P(('groups', 'cells')), parts along dimension 0
- grad_up: float32 [768, 1536], P(('groups', 'cells')), parts along dimension 0
- grad_down: float32 [3072, 384], P(('groups', 'cells')), parts along dimension 0
There are 2 independent parts, one for each index of `groups`. A program takes and returns all parts, laid end to end along the dimension named above; an argument that names none is the same for every part. Nothing has to cross between parts.
Inputs may be any that keep to these rules, and one draw needn't show every extreme that they name: `node_mask`: patch slot s of cell c (global id c * 3 + s) is live where s is below the cell's live count, which is 1 to 3, and 3 in the last cell ; empty slots hold only zeros, and the first node of every live patch is 1. `neighbours`: every id names a live patch of a cell at most 2 cells from the patch's own. Slot 0 names the patch itself where it is live, else slot 0 of its cell; slots 1, 2, 3, 4 name patches of the cells at offsets +1, -1, +2, -2, clipped to the first and last cell.
All inputs are finite; a program needn't handle non-finite values.
Results may differ from a plain program's by a relative error of at most 0.017.
Values may be sent and summed in bfloat16 or wider, within the bound.
A program may use at most 128 MiB of HBM per device.

v0:
```python
import jax
import jax.numpy as jnp
from jax import lax
from jax.sharding import PartitionSpec as P

D = 384
HEADS = 8
PATCH_NODES = 128
NEAR = 8


epsilon = 1e-06
score_scale = 5.0
block_patches = 3


def shifted(value, axis, steps):
    count = lax.axis_size(axis)
    initial, last = (max(0, -steps), min(count, count - steps))
    return lax.ppermute(value, axis, [(source, source + steps) for source in range(initial, last)])


def rms_rows(rows):
    return rows * lax.rsqrt(jnp.mean(rows * rows, axis=-1, keepdims=True) + epsilon)


def head_norm(rows):
    count = rows.shape[0]
    split = rows.reshape(count, HEADS, D // HEADS)
    split = split * lax.rsqrt(jnp.mean(split * split, axis=-1, keepdims=True) + epsilon)
    return split.reshape(count, D)


def head_major(rows):
    patches = rows.shape[0] // PATCH_NODES
    return rows.reshape(patches, PATCH_NODES, HEADS, D // HEADS).transpose(0, 2, 3, 1)


def row_major(tiles):
    patches = tiles.shape[0]
    return (
        tiles.reshape(patches, HEADS, D // HEADS, PATCH_NODES)
        .transpose(0, 3, 1, 2)
        .reshape(patches * PATCH_NODES, D)
    )


def probabilities(query_block, near_keys, near_weights):
    scores = jnp.einsum(
        "bhdi,bshdp->bhisp", query_block, near_keys, preferred_element_type=jnp.float32
    ) * (score_scale / (D // HEADS))
    raised = jnp.exp(scores) * near_weights[:, None, None, :, :]
    return raised / jnp.sum(raised, axis=(3, 4), keepdims=True)


def per_device(
    features,
    cotangent,
    inner_weight,
    outer_weight,
    upward_weight,
    downward_weight,
    node_mask,
    neighbours,
):
    count = features.shape[0]
    patches = count // PATCH_NODES
    head_size = D // HEADS
    blocks = patches // block_patches
    window_count = 5 * patches
    position = lax.axis_index("cells")
    inputs = features.astype(jnp.float32)
    normed = rms_rows(inputs).astype(jnp.bfloat16)
    projected = jnp.dot(normed, inner_weight, preferred_element_type=jnp.float32)
    raw_queries = projected[:, :D]
    raw_keys = projected[:, D : 2 * D]
    queries = head_norm(raw_queries).astype(jnp.bfloat16)
    keys = head_norm(raw_keys).astype(jnp.bfloat16)
    values = projected[:, 2 * D :].astype(jnp.bfloat16)
    own_parts = (head_major(keys), head_major(values), node_mask.astype(jnp.bfloat16))
    arrived = {}
    for offset in (2, 1, -1, -2):
        arrived[offset] = shifted((own_parts[0], own_parts[1], own_parts[2]), "cells", offset)
    ordered = [arrived[2], arrived[1], own_parts, arrived[-1], arrived[-2]]
    window_keys = jnp.concatenate([member[0] for member in ordered], axis=0)
    window_values = jnp.concatenate([member[1] for member in ordered], axis=0)
    window_weights = jnp.concatenate([member[2] for member in ordered], axis=0).astype(jnp.float32)
    local_index = neighbours - (position - 2) * patches
    query_blocks = head_major(queries).reshape(blocks, block_patches, HEADS, head_size, PATCH_NODES)
    index_blocks = local_index.reshape(blocks, block_patches, NEAR)

    def near_of(index_block):
        flat = index_block.reshape(-1)
        near_keys = jnp.take(window_keys, flat, axis=0).reshape(
            block_patches, NEAR, HEADS, head_size, PATCH_NODES
        )
        near_values = jnp.take(window_values, flat, axis=0).reshape(
            block_patches, NEAR, HEADS, head_size, PATCH_NODES
        )
        near_weights = jnp.take(window_weights, flat, axis=0).reshape(
            block_patches, NEAR, PATCH_NODES
        )
        return (near_keys, near_values, near_weights)

    def forward_block(pair):
        query_block, index_block = pair
        near_keys, near_values, near_weights = near_of(index_block)
        probs = probabilities(query_block, near_keys, near_weights)
        mixed = jnp.einsum(
            "bhisp,bshdp->bihd",
            probs.astype(jnp.bfloat16),
            near_values,
            preferred_element_type=jnp.float32,
        )
        return mixed.reshape(block_patches, PATCH_NODES, D).astype(jnp.bfloat16)

    attended = lax.map(forward_block, (query_blocks, index_blocks)).reshape(count, D)
    residual = (
        inputs + jnp.dot(attended, outer_weight, preferred_element_type=jnp.float32)
    ).astype(jnp.bfloat16)
    middle = residual.astype(jnp.float32)
    second = rms_rows(middle).astype(jnp.bfloat16)
    before = jnp.dot(second, upward_weight, preferred_element_type=jnp.float32)
    hidden = jax.nn.gelu(before).astype(jnp.bfloat16)
    back_hidden = jnp.dot(cotangent, downward_weight.T, preferred_element_type=jnp.float32)
    unused, gelu_back = jax.vjp(jax.nn.gelu, before)
    back_before = gelu_back(back_hidden)[0].astype(jnp.bfloat16)
    term_down = jnp.dot(hidden.T, cotangent, preferred_element_type=jnp.float32)
    term_up = jnp.dot(second.T, back_before, preferred_element_type=jnp.float32)
    back_second = jnp.dot(back_before, upward_weight.T, preferred_element_type=jnp.float32)
    unused, middle_back = jax.vjp(rms_rows, middle)
    back_residual = (cotangent.astype(jnp.float32) + middle_back(back_second)[0]).astype(
        jnp.bfloat16
    )
    back_attended = jnp.dot(
        back_residual, outer_weight.T, preferred_element_type=jnp.float32
    ).astype(jnp.bfloat16)
    term_outer = jnp.dot(attended.T, back_residual, preferred_element_type=jnp.float32)
    back_blocks = head_major(back_attended).reshape(
        blocks, block_patches, HEADS, head_size, PATCH_NODES
    )

    def backward_block(triple):
        query_block, index_block, back_block = triple
        near_keys, near_values, near_weights = near_of(index_block)
        probs = probabilities(query_block, near_keys, near_weights)
        back_probs = jnp.einsum(
            "bhdi,bshdp->bhisp", back_block, near_values, preferred_element_type=jnp.float32
        )
        back_scores = (
            probs
            * (back_probs - jnp.sum(probs * back_probs, axis=(3, 4), keepdims=True))
            * (score_scale / head_size)
        )
        scores_low = back_scores.astype(jnp.bfloat16)
        back_queries = jnp.einsum(
            "bhisp,bshdp->bihd", scores_low, near_keys, preferred_element_type=jnp.float32
        ).reshape(block_patches * PATCH_NODES, D)
        back_keys = jnp.einsum(
            "bhisp,bhdi->bshdp", scores_low, query_block, preferred_element_type=jnp.float32
        ).reshape(block_patches * NEAR, D * PATCH_NODES)
        back_values = jnp.einsum(
            "bhisp,bhdi->bshdp",
            probs.astype(jnp.bfloat16),
            back_block,
            preferred_element_type=jnp.float32,
        ).reshape(block_patches * NEAR, D * PATCH_NODES)
        return (back_queries, back_keys, back_values)

    back_queries, key_terms, value_terms = lax.map(
        backward_block, (query_blocks, index_blocks, back_blocks)
    )
    back_queries = back_queries.reshape(count, D)
    tile_ids = jnp.arange(window_count, dtype=jnp.int32)
    selector = (local_index.reshape(-1)[:, None] == tile_ids[None, :]).astype(jnp.float32)
    key_sums = jnp.einsum(
        "sw,sz->wz",
        selector,
        key_terms.reshape(patches * NEAR, D * PATCH_NODES),
        precision=lax.Precision.HIGHEST,
    )
    value_sums = jnp.einsum(
        "sw,sz->wz",
        selector,
        value_terms.reshape(patches * NEAR, D * PATCH_NODES),
        precision=lax.Precision.HIGHEST,
    )
    key_parts = key_sums.reshape(5, patches, D * PATCH_NODES)
    value_parts = value_sums.reshape(5, patches, D * PATCH_NODES)
    own_keys = key_parts[2]
    own_values = value_parts[2]
    for offset in (-2, -1, 1, 2):
        returned = (
            shifted(key_parts[offset + 2].astype(jnp.bfloat16), "cells", offset).astype(
                jnp.float32
            ),
            shifted(value_parts[offset + 2].astype(jnp.bfloat16), "cells", offset).astype(
                jnp.float32
            ),
        )
        own_keys = own_keys + returned[0]
        own_values = own_values + returned[1]
    unused, query_back = jax.vjp(head_norm, raw_queries)
    unused, key_back = jax.vjp(head_norm, raw_keys)
    back_projected = jnp.concatenate(
        [query_back(back_queries)[0], key_back(row_major(own_keys))[0], row_major(own_values)],
        axis=-1,
    ).astype(jnp.bfloat16)
    term_inner = jnp.dot(normed.T, back_projected, preferred_element_type=jnp.float32)
    back_normed = jnp.dot(back_projected, inner_weight.T, preferred_element_type=jnp.float32)
    unused, input_back = jax.vjp(rms_rows, inputs)
    back_features = (back_residual.astype(jnp.float32) + input_back(back_normed)[0]).astype(
        jnp.bfloat16
    )
    summed_inner, summed_outer, summed_up, summed_down = (
        lax.psum_scatter(term_inner, "cells", scatter_dimension=0, tiled=True),
        lax.psum_scatter(term_outer, "cells", scatter_dimension=0, tiled=True),
        lax.psum_scatter(term_up, "cells", scatter_dimension=0, tiled=True),
        lax.psum_scatter(term_down, "cells", scatter_dimension=0, tiled=True),
    )
    factor = (lax.axis_size("cells") * count) ** (-0.5)
    return (
        back_features,
        summed_inner * factor,
        summed_outer * factor,
        summed_up * factor,
        summed_down * factor,
    )


def solution(mesh):
    placed = (
        P(("groups", "cells"), None),
        P(("groups", "cells"), None),
        P(),
        P(),
        P(),
        P(),
        P(("groups", "cells"), None),
        P(("groups", "cells"), None),
    )
    return jax.shard_map(
        per_device,
        mesh=mesh,
        in_specs=placed,
        out_specs=(
            P(("groups", "cells"), None),
            P(("groups", "cells"), None),
            P(("groups", "cells"), None),
            P(("groups", "cells"), None),
            P(("groups", "cells"), None),
        ),
        check_vma=False,
    )
```

profile of v0, /device:TPU:0, one launch (start us, length us, event | category | flops | bytes accessed | tf_op | source)
XLA Modules:
  0.0 450.9 jit_solution(10858502791959769147)
XLA Ops:
  8.0 1.3 collective-permute-start.11
  9.3 1.3 collective-permute-start.10
  10.6 3.6 collective-permute-start.9
  14.2 5.6 %collective-permute-start.8 = (bf16[3,128]{1,0:T(4,128)(2,1)S(1)}, bf16[3,128]{1,0:T(4,128)(2,1)}, u32[]{:S(2)}, u32[]{:S(2)}) collective-permute-start(bf16[3,128]{1,0:T(4,128)(2,1)S(1)} %convert_element_type.109), channel_id=1, source_target_pairs={{0,2},{1,3},{2,4},{3,5},{4,6},{5,7},{6,8},{7,9},{8,10},{9,11},{10,... | collective-permute-start | bytes 2312 | tf_op jit(solution)/shard_map/ppermute | solution.py:20
  22.2 1.9 fusion.68
  24.1 1.6 reshape.262
  25.6 2.2 copy.106
  27.8 5.0 %collective-permute-start = (bf16[3,8,48,128]{3,2,1,0:T(8,128)(2,1)}, bf16[3,8,48,128]{3,2,1,0:T(8,128)(2,1)}, u32[]{:S(2)}, u32[]{:S(2)}) collective-permute-start(bf16[3,8,48,128]{3,2,1,0:T(8,128)(2,1)} %bitcast), channel_id=1, source_target_pairs={{0,2},{1,3},{2,4},{3,5},{4,6},{5,7},{6,8},{7,9},{8,10},{9,11},{10,... | collective-permute-start | bytes 884744 | tf_op jit(solution)/shard_map/ppermute | solution.py:20
  34.5 1.3 copy.107
  37.5 2.1 copy.108
  39.6 1.3 copy.110
  42.6 2.1 copy.111
  44.7 2.3 multiply_convert_fusion.5
  47.1 2.2 fusion.99
  52.4 1.3 collective-permute-start.3
  53.7 1.3 collective-permute-start.2
  55.0 3.0 collective-permute-start.1
  58.1 1.3 collective-permute-start.7
  59.4 1.4 concatenate.15
  61.5 1.3 collective-permute-start.6
  63.7 19.2 %collective-permute-start.4 = (bf16[3,8,48,128]{3,2,1,0:T(8,128)(2,1)S(1)}, bf16[3,8,48,128]{3,2,1,0:T(8,128)(2,1)S(1)}, u32[]{:S(2)}, u32[]{:S(2)}) collective-permute-start(bf16[3,8,48,128]{3,2,1,0:T(8,128)(2,1)S(1)} %bitcast.134), channel_id=1, source_target_pairs={{0,2},{1,3},{2,4},{3,5},{4,6},{5,7},{6,8},{7,9},{8,10},{9,11},{10,... | collective-permute-start | bytes 884744 | tf_op jit(solution)/shard_map/ppermute | solution.py:20
  84.0 3.2 collective-permute-done.4
  87.2 1.3 collective-permute-start.5
  90.7 3.7 gather_fusion
  95.6 2.4 gather_fusion.1
  98.0 2.9 broadcast_select_fusion
  100.9 4.3 fusion.1
  105.3 3.4 fusion.40
  108.7 1.8 copy-done.2
  111.2 3.5 fusion.12
  118.7 7.9 %fusion.13 = f32[3,8,8,48,128]{4,3,1,2,0:T(8,128)} fusion(bf16[3,8,48,128,1]{3,0,2,1,4:T(4,128)(2,1)} %bitcast.137, f32[3,8,128,8,128]{2,4,3,1,0:T(8,128)} %copy-done.2, f32[3,8,128]{2,1,0:T(8,128)S(1)} %copy-done.44, f32[3,8,128]{2,1,0:T(8,128)S(1)} %select_bitcast_fusion), kind=kOutput, calls=%fused_computation.24 | convolution fusion | flops 314572800 | bytes 17620992 | tf_op jit(solution)/shard_map/while/body/eval_jaxpr/bhisp,bhdi->bshdp/dot_general | solution.py:162
  126.6 12.8 %multiply_reduce_fusion = (f32[3,8,128]{2,1,0:T(8,128)S(1)}, f32[3,8,128,8,128]{2,4,3,1,0:T(8,128)}) fusion(f32[3,8,128]{2,1,0:T(8,128)S(1)} %copy-done.44, f32[3,8,128]{2,1,0:T(8,128)S(1)} %select_bitcast_fusion, f32[3,8,128,8,128]{2,4,3,1,0:T(8,128)} %copy-done.2, bf16[3,8,8,48,128]{4,3,2,1,0:T(8,128)(2,1)S(1)} %bitcast.130, ...), kind=kOutput, calls=%fused_computation.4 | convolution fusion | flops 317715456 | bytes 27856896 | tf_op jit(solution)/shard_map/while/body/eval_jaxpr/bhdi,bshdp->bhisp/dot_general | solution.py:147
  139.4 7.6 %multiply_convert_fusion = bf16[3,8,128,8,128]{2,4,3,1,0:T(8,128)(2,1)S(1)} fusion(f32[3,8,128,8,128]{2,4,3,1,0:T(8,128)} %get-tuple-element.105, f32[3,8,128]{2,1,0:T(8,128)S(1)} %get-tuple-element.104, f32[3,8,128]{2,1,0:T(8,128)S(1)} %copy-done.44, f32[3,8,128]{2,1,0:T(8,128)S(1)} %select_bitcast_fusion, f32[3,8,128,8,128]{2,4,3,1,0:T(8,128)S(1)} %bitcast.108), kind=kLoop, calls=%fused_computation.3 | loop fusion | flops 22020096 | bytes 31494144 | tf_op jit(solution)/shard_map/while/body/eval_jaxpr/convert_element_type | solution.py:155
  148.3 4.5 convolution_bitcast_fusion
  152.8 5.2 %copy.138 = f32[3,8,8,48,128]{4,3,2,1,0:T(8,128)} copy(f32[3,8,8,48,128]{4,3,1,2,0:T(8,128)} %fusion.13) | data formatting | bytes 9437184 | tf_op jit(solution)/shard_map/while/body/eval_jaxpr/bhisp,bhdi->bshdp/transpose | solution.py:162
  158.0 5.8 %reshape.220 = f32[24,49152]{1,0:T(8,128)} reshape(f32[3,8,8,48,128]{4,3,2,1,0:T(8,128)} %copy.138) | data formatting | bytes 9437184 | tf_op jit(solution)/shard_map/reshape | solution.py:185
  163.8 5.3 %fusion.97 = (bf16[15,49152]{1,0:T(8,128)(2,1)S(1)}, f32[15,49152]{1,0:T(8,128)}) fusion(f32[24,49152]{1,0:T(8,128)} %reshape.220, s32[24]{0:T(128)S(1)} %copy-done.50), kind=kOutput, calls=%fused_computation.144 | convolution fusion | flops 213074272 | bytes 9142368 | tf_op jit(solution)/shard_map/sw,sz->wz/dot_general | solution.py:182
  169.1 1.5 fusion.96
  171.9 2.8 copy.131
  174.7 5.8 %reshape.218 = f32[24,49152]{1,0:T(8,128)} reshape(f32[3,8,8,48,128]{4,3,2,1,0:T(8,128)} %copy.131) | data formatting | bytes 9437184 | tf_op jit(solution)/shard_map/reshape | solution.py:179
  180.4 5.1 %fusion.98 = (bf16[15,49152]{1,0:T(8,128)(2,1)S(1)}, f32[15,49152]{1,0:T(8,128)}) fusion(f32[24,49152]{1,0:T(8,128)} %reshape.218, s32[24]{0:T(128)S(1)} %copy-done.50), kind=kOutput, calls=%fused_computation.145 | convolution fusion | flops 213074272 | bytes 9142368 | tf_op jit(solution)/shard_map/sw,sz->wz/dot_general | solution.py:176
  185.5 1.7 fusion.95
  188.5 11.4 %collective-permute-start.15 = (bf16[3,49152]{1,0:T(4,128)(2,1)}, bf16[3,49152]{1,0:T(4,128)(2,1)}, u32[]{:S(2)}, u32[]{:S(2)}) collective-permute-start(bf16[3,49152]{1,0:T(4,128)(2,1)} %get-tuple-element.85), channel_id=1, source_target_pairs={{0,2},{1,3},{2,4},{3,5},{4,6},{5,7},{6,8},{7,9},{8,10},{9,11},{10,... | collective-permute-start | bytes 884744 | tf_op jit(solution)/shard_map/ppermute | solution.py:20
  199.9 3.4 collective-permute-start.14
  206.4 1.3 reshape.264
  207.7 6.4 %collective-permute-start.19 = (bf16[3,49152]{1,0:T(4,128)(2,1)S(1)}, bf16[3,49152]{1,0:T(4,128)(2,1)S(1)}, u32[]{:S(2)}, u32[]{:S(2)}) collective-permute-start(bf16[3,49152]{1,0:T(4,128)(2,1)S(1)} %copy-done.33), channel_id=1, source_target_pairs={{0,2},{1,3},{2,4},{3,5},{4,6},{5,7},{6,8},{7,9},{8,10},{9,11},{10,... | collective-permute-start | bytes 884744 | tf_op jit(solution)/shard_map/ppermute | solution.py:20
  214.1 7.0 %collective-permute-done.15 = bf16[3,49152]{1,0:T(4,128)(2,1)} collective-permute-done((bf16[3,49152]{1,0:T(4,128)(2,1)}, bf16[3,49152]{1,0:T(4,128)(2,1)}, u32[]{:S(2)}, u32[]{:S(2)}) %collective-permute-start.15) | collective-permute-done | bytes 294944 | tf_op jit(solution)/shard_map/ppermute | solution.py:20
  221.0 2.8 collective-permute-start.18
  223.8 1.5 collective-permute-start.17
  225.4 2.8 fusion.51
  229.3 3.5 collective-permute-done.17
  232.8 2.8 fusion.48
  237.5 2.0 fusion.54
  240.2 1.9 fusion.62
  242.2 4.2 fusion.35
  247.9 2.2 fusion.76
  250.2 2.0 fusion.60
  253.2 1.4 broadcast_multiply_fusion.3
  254.6 56.4 %reduce-scatter.13.cloned.1.call-done = f32[24,1152]{1,0:T(8,128)} async-done(((f32[384,1152]{1,0:T(8,128)}), f32[24,1152]{1,0:T(8,128)}) %reduce-scatter.13.cloned.1.call-update) | async-done | bytes 110608
  311.0 1.6 broadcast_multiply_fusion.2
  312.5 64.6 %reduce-scatter.11.cloned.1.call-done = f32[96,384]{1,0:T(8,128)} async-done(((f32[1536,384]{1,0:T(8,128)}), f32[96,384]{1,0:T(8,128)}) %reduce-scatter.11.cloned.1.call-update) | async-done | bytes 147472 | tf_op jit(solution)/shard_map/reduce_scatter | solution.py:219
  377.2 1.6 broadcast_multiply_fusion
  378.7 64.0 %reduce-scatter.9.cloned.1.call-done = f32[24,1536]{1,0:T(8,128)} async-done(((f32[384,1536]{1,0:T(8,128)}), f32[24,1536]{1,0:T(8,128)}) %reduce-scatter.9.cloned.1.call-update) | async-done | bytes 147472 | tf_op jit(solution)/shard_map/reduce_scatter | solution.py:218
  442.8 1.6 broadcast_multiply_fusion.1
  (209 shorter events, 35.3 us)
Async XLA Ops:
  7.2 104.1 %copy-start = (bf16[384,1536]{1,0:T(8,128)(2,1)S(1)}, bf16[384,1536]{1,0:T(8,128)(2,1)}, u32[]{:S(2)}) copy-start(bf16[384,1536]{1,0:T(8,128)(2,1)} %param.16) | copy-start | bytes 3538948
  7.2 246.1 %reduce-scatter.15.cloned.1.call-start = ((), (), s32[]{:S(2)}) async-start(), calls=%async_computation.7 | async-start | bytes 626688
  8.0 44.4 %collective-permute-start.11 = (bf16[3,128]{1,0:T(4,128)(2,1)S(1)}, bf16[3,128]{1,0:T(4,128)(2,1)S(1)}, u32[]{:S(2)}, u32[]{:S(2)}) collective-permute-start(bf16[3,128]{1,0:T(4,128)(2,1)S(1)} %convert_element_type.109), channel_id=1, source_target_pairs={{2,0},{3,1},{4,2},{5,3},{6,4},{7,5},{8,6},{9,7},{10,8},{11,9},{12,... | collective-permute-start | bytes 2312 | tf_op jit(solution)/shard_map/ppermute | solution.py:20
  9.3 44.4 %collective-permute-start.10 = (bf16[3,128]{1,0:T(4,128)(2,1)S(1)}, bf16[3,128]{1,0:T(4,128)(2,1)}, u32[]{:S(2)}, u32[]{:S(2)}) collective-permute-start(bf16[3,128]{1,0:T(4,128)(2,1)S(1)} %convert_element_type.109), channel_id=1, source_target_pairs={{1,0},{2,1},{3,2},{4,3},{5,4},{6,5},{7,6},{8,7},{9,8},{10,9},{11,1... | collective-permute-start | bytes 2312 | tf_op jit(solution)/shard_map/ppermute | solution.py:20
  10.6 44.4 %collective-permute-start.9 = (bf16[3,128]{1,0:T(4,128)(2,1)S(1)}, bf16[3,128]{1,0:T(4,128)(2,1)}, u32[]{:S(2)}, u32[]{:S(2)}) collective-permute-start(bf16[3,128]{1,0:T(4,128)(2,1)S(1)} %convert_element_type.109), channel_id=1, source_target_pairs={{0,1},{1,2},{2,3},{3,4},{4,5},{5,6},{6,7},{7,8},{8,9},{9,10},{10,1... | collective-permute-start | bytes 2312 | tf_op jit(solution)/shard_map/ppermute | solution.py:20
  14.2 43.9 %collective-permute-start.8 = (bf16[3,128]{1,0:T(4,128)(2,1)S(1)}, bf16[3,128]{1,0:T(4,128)(2,1)}, u32[]{:S(2)}, u32[]{:S(2)}) collective-permute-start(bf16[3,128]{1,0:T(4,128)(2,1)S(1)} %convert_element_type.109), channel_id=1, source_target_pairs={{0,2},{1,3},{2,4},{3,5},{4,6},{5,7},{6,8},{7,9},{8,10},{9,11},{10,... | collective-permute-start | bytes 2312 | tf_op jit(solution)/shard_map/ppermute | solution.py:20
  20.9 4.8 %copy-start.7 = (bf16[384,384]{0,1:T(8,128)(2,1)}, bf16[384,384]{0,1:T(8,128)(2,1)S(1)}, u32[]{:S(2)}) copy-start(bf16[384,384]{0,1:T(8,128)(2,1)S(1)} %copy.104) | copy-start | bytes 884740
  22.2 10.7 %copy-start.52 = (s32[3,8]{1,0:T(4,128)S(1)}, s32[3,8]{1,0:T(4,128)}, u32[]{:S(2)}) copy-start(s32[3,8]{1,0:T(4,128)} %param.19) | copy-start | bytes 292
  24.0 20.7 %copy-start.3 = (f32[384,1152]{1,0:T(8,128)}, f32[384,1152]{1,0:T(8,128)S(1)}, u32[]{:S(2)}) copy-start(f32[384,1152]{1,0:T(8,128)S(1)} %fusion.68) | copy-start | bytes 5308420
  27.8 33.6 %collective-permute-start = (bf16[3,8,48,128]{3,2,1,0:T(8,128)(2,1)}, bf16[3,8,48,128]{3,2,1,0:T(8,128)(2,1)}, u32[]{:S(2)}, u32[]{:S(2)}) collective-permute-start(bf16[3,8,48,128]{3,2,1,0:T(8,128)(2,1)} %bitcast), channel_id=1, source_target_pairs={{0,2},{1,3},{2,4},{3,5},{4,6},{5,7},{6,8},{7,9},{8,10},{9,11},{10,... | collective-permute-start | bytes 884744 | tf_op jit(solution)/shard_map/ppermute | solution.py:20
  35.8 3.8 copy-start.14
  40.9 6.1 %copy-start.12 = (f32[384,384]{0,1:T(8,128)}, f32[384,384]{0,1:T(8,128)S(1)}, u32[]{:S(2)}) copy-start(f32[384,384]{0,1:T(8,128)S(1)} %copy.110) | copy-start | bytes 1769476
  44.7 2.3 copy-start.29
  44.7 2.3 copy-start.30
  47.0 2.2 copy-start.31
  47.0 3.1 copy-start.24
  47.1 4.2 copy-start.25
  49.3 12.1 %copy-start.51 = (pred[24]{0:T(512)(128)(4,1)S(1)}, pred[24]{0:T(512)(128)(4,1)}, u32[]{:S(2)}) copy-start(pred[24]{0:T(512)(128)(4,1)} %compare_and_fusion) | copy-start | bytes 76
  52.4 37.2 %collective-permute-start.3 = (bf16[3,8,48,128]{3,2,1,0:T(8,128)(2,1)}, bf16[3,8,48,128]{3,2,1,0:T(8,128)(2,1)S(1)}, u32[]{:S(2)}, u32[]{:S(2)}) collective-permute-start(bf16[3,8,48,128]{3,2,1,0:T(8,128)(2,1)} %bitcast), channel_id=1, source_target_pairs={{2,0},{3,1},{4,2},{5,3},{6,4},{7,5},{8,6},{9,7},{10,8},{11,9},{12,... | collective-permute-start | bytes 884744 | tf_op jit(solution)/shard_map/ppermute | solution.py:20
  53.7 34.8 %collective-permute-start.2 = (bf16[3,8,48,128]{3,2,1,0:T(8,128)(2,1)}, bf16[3,8,48,128]{3,2,1,0:T(8,128)(2,1)}, u32[]{:S(2)}, u32[]{:S(2)}) collective-permute-start(bf16[3,8,48,128]{3,2,1,0:T(8,128)(2,1)} %bitcast), channel_id=1, source_target_pairs={{1,0},{2,1},{3,2},{4,3},{5,4},{6,5},{7,6},{8,7},{9,8},{10,9},{11,1... | collective-permute-start | bytes 884744 | tf_op jit(solution)/shard_map/ppermute | solution.py:20
  55.0 8.8 %collective-permute-start.1 = (bf16[3,8,48,128]{3,2,1,0:T(8,128)(2,1)}, bf16[3,8,48,128]{3,2,1,0:T(8,128)(2,1)S(1)}, u32[]{:S(2)}, u32[]{:S(2)}) collective-permute-start(bf16[3,8,48,128]{3,2,1,0:T(8,128)(2,1)} %bitcast), channel_id=1, source_target_pairs={{0,1},{1,2},{2,3},{3,4},{4,5},{5,6},{6,7},{7,8},{8,9},{9,10},{10,1... | collective-permute-start | bytes 884744 | tf_op jit(solution)/shard_map/ppermute | solution.py:20
  58.1 37.5 %collective-permute-start.7 = (bf16[3,8,48,128]{3,2,1,0:T(8,128)(2,1)S(1)}, bf16[3,8,48,128]{3,2,1,0:T(8,128)(2,1)S(1)}, u32[]{:S(2)}, u32[]{:S(2)}) collective-permute-start(bf16[3,8,48,128]{3,2,1,0:T(8,128)(2,1)S(1)} %bitcast.132), channel_id=1, source_target_pairs={{2,0},{3,1},{4,2},{5,3},{6,4},{7,5},{8,6},{9,7},{10,8},{11,9},{12,... | collective-permute-start | bytes 884744 | tf_op jit(solution)/shard_map/ppermute | solution.py:20
  61.5 33.0 %collective-permute-start.6 = (bf16[3,8,48,128]{3,2,1,0:T(8,128)(2,1)S(1)}, bf16[3,8,48,128]{3,2,1,0:T(8,128)(2,1)}, u32[]{:S(2)}, u32[]{:S(2)}) collective-permute-start(bf16[3,8,48,128]{3,2,1,0:T(8,128)(2,1)S(1)} %bitcast.133), channel_id=1, source_target_pairs={{1,0},{2,1},{3,2},{4,3},{5,4},{6,5},{7,6},{8,7},{9,8},{10,9},{11,1... | collective-permute-start | bytes 884744 | tf_op jit(solution)/shard_map/ppermute | solution.py:20
  63.7 23.4 %collective-permute-start.4 = (bf16[3,8,48,128]{3,2,1,0:T(8,128)(2,1)S(1)}, bf16[3,8,48,128]{3,2,1,0:T(8,128)(2,1)S(1)}, u32[]{:S(2)}, u32[]{:S(2)}) collective-permute-start(bf16[3,8,48,128]{3,2,1,0:T(8,128)(2,1)S(1)} %bitcast.134), channel_id=1, source_target_pairs={{0,2},{1,3},{2,4},{3,5},{4,6},{5,7},{6,8},{7,9},{8,10},{9,11},{10,... | collective-permute-start | bytes 884744 | tf_op jit(solution)/shard_map/ppermute | solution.py:20
  87.2 3.5 collective-permute-start.5
  98.0 2.9 copy-start.19
  100.9 4.4 copy-start.22
  105.2 5.2 %copy-start.2 = (f32[3,8,128,8,128]{2,4,3,1,0:T(8,128)}, f32[3,8,128,8,128]{2,4,3,1,0:T(8,128)S(1)}, u32[]{:S(2)}) copy-start(f32[3,8,128,8,128]{2,4,3,1,0:T(8,128)S(1)} %get-tuple-element.95) | copy-start | bytes 37748740
  105.2 5.2 %copy-start.43 = (f32[3,8,128]{2,1,0:T(8,128)}, f32[3,8,128]{2,1,0:T(8,128)S(1)}, u32[]{:S(2)}) copy-start(f32[3,8,128]{2,1,0:T(8,128)S(1)} %get-tuple-element.94) | copy-start | bytes 36868
  105.3 5.5 %copy-start.8 = (bf16[384,384]{0,1:T(8,128)(2,1)S(1)}, bf16[384,384]{0,1:T(8,128)(2,1)}, u32[]{:S(2)}) copy-start(bf16[384,384]{0,1:T(8,128)(2,1)} %copy-done.7) | copy-start | bytes 884740
  105.3 5.5 %copy-start.27 = (bf16[384,384]{1,0:T(8,128)(2,1)S(1)}, bf16[384,384]{1,0:T(8,128)(2,1)}, u32[]{:S(2)}) copy-start(bf16[384,384]{1,0:T(8,128)(2,1)} %param.15) | copy-start | bytes 884740
  105.3 5.9 %copy-start.21 = (f32[384,1536]{1,0:T(8,128)S(1)}, f32[384,1536]{1,0:T(8,128)}, u32[]{:S(2)}) copy-start(f32[384,1536]{1,0:T(8,128)} %fusion.99) | copy-start | bytes 7077892
  111.2 4.3 copy-start.5
  115.8 2.8 copy-start.44
  116.0 10.5 %copy-start.17 = (bf16[384,384]{0,1:T(8,128)(2,1)}, bf16[384,384]{0,1:T(8,128)(2,1)S(1)}, u32[]{:S(2)}) copy-start(bf16[384,384]{0,1:T(8,128)(2,1)S(1)} %fusion.53) | copy-start | bytes 884740
  118.7 7.9 %copy-start.23 = (bf16[24,8,48,128]{3,2,1,0:T(8,128)(2,1)S(1)}, bf16[24,8,48,128]{3,2,1,0:T(8,128)(2,1)}, u32[]{:S(2)}) copy-start(bf16[24,8,48,128]{3,2,1,0:T(8,128)(2,1)} %copy-done.22) | copy-start | bytes 7077892
  118.7 7.9 %copy-start.34 = (bf16[3,128,8,48]{1,0,3,2:T(4,128)(2,1)S(1)}, bf16[3,128,8,48]{1,0,3,2:T(4,128)(2,1)}, u32[]{:S(2)}) copy-start(bf16[3,128,8,48]{1,0,3,2:T(4,128)(2,1)} %reshape.217) | copy-start | bytes 884740
  118.7 20.7 %slice-start = ((s8[12582912]{0:T(1024)(128)(4,1)}), s8[4194304]{0:T(1024)(128)(4,1)S(1)}, s32[]{:S(2)}) async-start(s8[12582912]{0:T(1024)(128)(4,1)} %bitcast.107), calls=%async_computation.8 | async-start | bytes 8388608
  118.7 20.7 %slice-start.1 = ((s8[12582912]{0:T(1024)(128)(4,1)}), s8[4194304]{0:T(1024)(128)(4,1)S(1)}, s32[]{:S(2)}) async-start(s8[12582912]{0:T(1024)(128)(4,1)} %bitcast.107), calls=%async_computation.9 | async-start | bytes 8388608
  126.6 12.8 %slice-start.2 = ((s8[12582912]{0:T(1024)(128)(4,1)}), s8[4194304]{0:T(1024)(128)(4,1)S(1)}, s32[]{:S(2)}) async-start(s8[12582912]{0:T(1024)(128)(4,1)} %bitcast.107), calls=%async_computation.10 | async-start | bytes 8388608
  152.8 158.2 %reduce-scatter.13.cloned.1.call-start = ((), (), s32[]{:S(2)}) async-start(), calls=%async_computation.6 | async-start | bytes 1880064
  158.0 5.8 %copy-start.50 = (s32[24]{0:T(128)S(1)}, s32[24]{0:T(128)}, u32[]{:S(2)}) copy-start(s32[24]{0:T(128)} %copy-done.49) | copy-start | bytes 292
  158.0 13.9 %slice-start.3 = ((s8[4718592]{0:T(1024)(128)(4,1)}), s8[524288]{0:T(1024)(128)(4,1)S(1)}, s32[]{:S(2)}) async-start(s8[4718592]{0:T(1024)(128)(4,1)} %bitcast.109), calls=%async_computation.11 | async-start | bytes 1048576
  163.8 8.1 %slice-start.4 = ((s8[4718592]{0:T(1024)(128)(4,1)}), s8[4194304]{0:T(1024)(128)(4,1)S(1)}, s32[]{:S(2)}) async-start(s8[4718592]{0:T(1024)(128)(4,1)} %bitcast.109), calls=%async_computation.12 | async-start | bytes 8388608
  170.6 58.0 %collective-permute-start.16 = (bf16[3,49152]{1,0:T(4,128)(2,1)}, bf16[3,49152]{1,0:T(4,128)(2,1)}, u32[]{:S(2)}, u32[]{:S(2)}) collective-permute-start(bf16[3,49152]{1,0:T(4,128)(2,1)} %get-tuple-element.88), channel_id=1, source_target_pairs={{2,0},{3,1},{4,2},{5,3},{6,4},{7,5},{8,6},{9,7},{10,8},{11,9},{12,... | collective-permute-start | bytes 884744 | tf_op jit(solution)/shard_map/ppermute | solution.py:20
  185.5 19.1 %copy-start.15 = (f32[384,384]{0,1:T(8,128)S(1)}, f32[384,384]{0,1:T(8,128)}, u32[]{:S(2)}) copy-start(f32[384,384]{0,1:T(8,128)} %copy-done.14) | copy-start | bytes 1769476
  185.5 19.2 %copy-start.42 = (f32[384,8]{0,1:T(8,128)S(1)}, f32[384,8]{0,1:T(8,128)}, u32[]{:S(2)}) copy-start(f32[384,8]{0,1:T(8,128)} %copy-done.41) | copy-start | bytes 36868
  187.2 20.5 %collective-permute-start.12 = (bf16[3,49152]{1,0:T(4,128)(2,1)}, bf16[3,49152]{1,0:T(4,128)(2,1)}, u32[]{:S(2)}, u32[]{:S(2)}) collective-permute-start(bf16[3,49152]{1,0:T(4,128)(2,1)} %get-tuple-element.84), channel_id=1, source_target_pairs={{2,0},{3,1},{4,2},{5,3},{6,4},{7,5},{8,6},{9,7},{10,8},{11,9},{12,... | collective-permute-start | bytes 884744 | tf_op jit(solution)/shard_map/ppermute | solution.py:20
  188.5 32.5 %collective-permute-start.15 = (bf16[3,49152]{1,0:T(4,128)(2,1)}, bf16[3,49152]{1,0:T(4,128)(2,1)}, u32[]{:S(2)}, u32[]{:S(2)}) collective-permute-start(bf16[3,49152]{1,0:T(4,128)(2,1)} %get-tuple-element.85), channel_id=1, source_target_pairs={{0,2},{1,3},{2,4},{3,5},{4,6},{5,7},{6,8},{7,9},{8,10},{9,11},{10,... | collective-permute-start | bytes 884744 | tf_op jit(solution)/shard_map/ppermute | solution.py:20
  199.9 23.9 %collective-permute-start.14 = (bf16[3,49152]{1,0:T(4,128)(2,1)}, bf16[3,49152]{1,0:T(4,128)(2,1)}, u32[]{:S(2)}, u32[]{:S(2)}) collective-permute-start(bf16[3,49152]{1,0:T(4,128)(2,1)} %get-tuple-element.86), channel_id=1, source_target_pairs={{0,1},{1,2},{2,3},{3,4},{4,5},{5,6},{6,7},{7,8},{8,9},{9,10},{10,1... | collective-permute-start | bytes 884744 | tf_op jit(solution)/shard_map/ppermute | solution.py:20
  203.3 22.1 %collective-permute-start.13 = (bf16[3,49152]{1,0:T(4,128)(2,1)}, bf16[3,49152]{1,0:T(4,128)(2,1)}, u32[]{:S(2)}, u32[]{:S(2)}) collective-permute-start(bf16[3,49152]{1,0:T(4,128)(2,1)} %get-tuple-element.87), channel_id=1, source_target_pairs={{1,0},{2,1},{3,2},{4,3},{5,4},{6,5},{7,6},{8,7},{9,8},{10,9},{11,1... | collective-permute-start | bytes 884744 | tf_op jit(solution)/shard_map/ppermute | solution.py:20
  207.7 21.7 %collective-permute-start.19 = (bf16[3,49152]{1,0:T(4,128)(2,1)S(1)}, bf16[3,49152]{1,0:T(4,128)(2,1)S(1)}, u32[]{:S(2)}, u32[]{:S(2)}) collective-permute-start(bf16[3,49152]{1,0:T(4,128)(2,1)S(1)} %copy-done.33), channel_id=1, source_target_pairs={{0,2},{1,3},{2,4},{3,5},{4,6},{5,7},{6,8},{7,9},{8,10},{9,11},{10,... | collective-permute-start | bytes 884744 | tf_op jit(solution)/shard_map/ppermute | solution.py:20
  221.0 8.3 %collective-permute-start.18 = (bf16[3,49152]{1,0:T(4,128)(2,1)S(1)}, bf16[3,49152]{1,0:T(4,128)(2,1)}, u32[]{:S(2)}, u32[]{:S(2)}) collective-permute-start(bf16[3,49152]{1,0:T(4,128)(2,1)S(1)} %get-tuple-element.90), channel_id=1, source_target_pairs={{0,1},{1,2},{2,3},{3,4},{4,5},{5,6},{6,7},{7,8},{8,9},{9,10},{10,1... | collective-permute-start | bytes 884744 | tf_op jit(solution)/shard_map/ppermute | solution.py:20
  223.8 9.0 %collective-permute-start.17 = (bf16[3,49152]{1,0:T(4,128)(2,1)S(1)}, bf16[3,49152]{1,0:T(4,128)(2,1)}, u32[]{:S(2)}, u32[]{:S(2)}) collective-permute-start(bf16[3,49152]{1,0:T(4,128)(2,1)S(1)} %get-tuple-element.91), channel_id=1, source_target_pairs={{1,0},{2,1},{3,2},{4,3},{5,4},{6,5},{7,6},{8,7},{9,8},{10,9},{11,1... | collective-permute-start | bytes 884744 | tf_op jit(solution)/shard_map/ppermute | solution.py:20
  228.2 7.4 %copy-start.13 = (f32[384,384]{0,1:T(8,128)S(1)}, f32[384,384]{0,1:T(8,128)}, u32[]{:S(2)}) copy-start(f32[384,384]{0,1:T(8,128)} %copy-done.12) | copy-start | bytes 1769476
  232.8 3.1 copy-start.40
  235.9 3.6 copy-start.35
  237.5 2.8 copy-start.9
  237.5 2.8 copy-start.46
  242.1 135.0 %reduce-scatter.11.cloned.1.call-start = ((), (), s32[]{:S(2)}) async-start(), calls=%async_computation.5 | async-start | bytes 2506752 | tf_op jit(solution)/shard_map/reduce_scatter | solution.py:219
  246.4 3.7 copy-start.36
  246.4 3.7 copy-start.38
  246.5 196.3 %reduce-scatter.9.cloned.1.call-start = ((), (), s32[]{:S(2)}) async-start(), calls=%async_computation.4 | async-start | bytes 2506752 | tf_op jit(solution)/shard_map/reduce_scatter | solution.py:218
  250.2 194.2 %copy-start.1 = (bf16[384,1536]{1,0:T(8,128)(2,1)S(1)}, bf16[384,1536]{1,0:T(8,128)(2,1)}, u32[]{:S(2)}) copy-start(bf16[384,1536]{1,0:T(8,128)(2,1)} %param.16) | copy-start | bytes 3538948
  (18 other events, 23.5 us)
Sparse Core Ops, SparseCore 0:
  152.9 68.5 reduce-scatter.14
  242.2 68.6 reduce-scatter.12
  315.2 61.8 reduce-scatter.10
  380.8 61.9 reduce-scatter.8
where the time goes:
time: 453 us; the launch traced here: 451 us
  waiting for transfers between devices  200 us (44%)
  starting transfers between devices  74.9 us (17%)
  local copies, waits for them, and re-layouts  68.1 us (15%)
  matrix products  65 us (14%)
  other arithmetic  28.7 us (6%)
  between operations  14.8 us (3%)
    ppermute x20, starting transfers between devices, shifted(): lax.ppermute(value, axis, [(source, source + steps) for source in range(i...  74.7 us
    reduce_scatter x1, waiting for transfers between devices, per_device(): lax.psum_scatter(term_down, 'cells', scatter_dimension=0, tiled=True)  64.6 us
    reduce_scatter x1, waiting for transfers between devices, per_device(): lax.psum_scatter(term_up, 'cells', scatter_dimension=0, tiled=True)  64 us
    unnamed x6, waiting for transfers between devices  56.4 us
    unnamed x129, local copies, waits for them, and re-layouts  15.3 us
    ppermute x20, waiting for transfers between devices, shifted(): lax.ppermute(value, axis, [(source, source + steps) for source in range(i...  14.4 us
    dot_general x1, matrix products, backward_block(): jnp.einsum('bhdi,bshdp->bhisp', back_block, near_values, preferred_elemen...  12.8 us
  transfers between devices with their start and end apart: 24, of which 7 were waited for; matrix products, arithmetic and copies ran while one was open for 21% of the time, Pallas kernels for 0%

commit v1 on v0

v1 whole, which is shorter than its diff:
```python
import functools

import jax
import jax.numpy as jnp
from jax import lax
from jax.experimental import pallas as pl
from jax.experimental.pallas import tpu as pltpu
from jax.sharding import PartitionSpec as P

D = 384
HEADS = 8
PATCH_NODES = 128
NEAR = 8


epsilon = 1e-06
score_scale = 5.0


def rms_rows(rows):
    return rows * lax.rsqrt(jnp.mean(rows * rows, axis=-1, keepdims=True) + epsilon)


def head_norm(rows):
    count = rows.shape[0]
    split = rows.reshape(count, HEADS, D // HEADS)
    split = split * lax.rsqrt(jnp.mean(split * split, axis=-1, keepdims=True) + epsilon)
    return split.reshape(count, D)


HEAD = D // HEADS
VALUE_ROW = D
MASK_ROW = 2 * D
WINDOW_ROWS = 2 * D + 16
OFFSETS = (-1, 1, -2, 2)
MESH = pl.DeviceIdType.MESH
VMEM_LIMIT = 40 * 1024 * 1024


def whole():
    return pl.BlockSpec(memory_space=pltpu.VMEM)


def dot(left, right, left_dim, right_dim):
    return lax.dot_general(
        left, right, (((left_dim,), (right_dim,)), ((), ())), preferred_element_type=jnp.float32
    )


def head_major(rows):
    patches = rows.shape[0] // PATCH_NODES
    return rows.reshape(patches, PATCH_NODES, D).transpose(0, 2, 1)


def row_major(tiles):
    return tiles.transpose(0, 2, 1).reshape(tiles.shape[0] * PATCH_NODES, D)


def near_tiles(window_ref, ids, start, size):
    return jnp.concatenate([window_ref[one, start : start + size, :] for one in ids], axis=1)


def weights_of(window_ref, ids):
    return near_tiles(window_ref, ids, MASK_ROW, 16).astype(jnp.float32)[0:1, :]


def softmax(query, key, weights):
    raised = jnp.exp(dot(query, key, 0, 0) * (score_scale / HEAD)) * weights
    return raised * (1.0 / jnp.sum(raised, axis=1, keepdims=True))


def forward_kernel(index_ref, query_ref, window_ref, attended_ref):
    @pl.loop(0, query_ref.shape[0])
    def _(patch):
        ids = [index_ref[patch, slot] for slot in range(NEAR)]
        weights = weights_of(window_ref, ids)
        for head in range(HEADS):
            start = head * HEAD
            key = near_tiles(window_ref, ids, start, HEAD)
            value = near_tiles(window_ref, ids, VALUE_ROW + start, HEAD)
            query = query_ref[patch, start : start + HEAD, :]
            probs = softmax(query, key, weights).astype(jnp.bfloat16)
            attended_ref[patch, start : start + HEAD, :] = dot(value, probs, 1, 1).astype(
                jnp.bfloat16
            )


def backward_kernel(index_ref, query_ref, back_ref, window_ref, back_query_ref, sums_ref):
    sums_ref[...] = jnp.zeros_like(sums_ref)

    @pl.loop(0, query_ref.shape[0])
    def _(patch):
        ids = [index_ref[patch, slot] for slot in range(NEAR)]
        weights = weights_of(window_ref, ids)
        for head in range(HEADS):
            start = head * HEAD
            rows = slice(start, start + HEAD)
            value_rows = slice(VALUE_ROW + start, VALUE_ROW + start + HEAD)
            key = near_tiles(window_ref, ids, start, HEAD)
            value = near_tiles(window_ref, ids, VALUE_ROW + start, HEAD)
            query = query_ref[patch, rows, :]
            back = back_ref[patch, rows, :]
            probs = softmax(query, key, weights)
            weighted = probs * dot(back, value, 0, 0)
            total = jnp.sum(weighted, axis=1, keepdims=True)
            scores = ((weighted - probs * total) * (score_scale / HEAD)).astype(jnp.bfloat16)
            back_query_ref[patch, rows, :] = dot(key, scores, 1, 1)
            back_key = dot(query, scores, 1, 0)
            back_value = dot(back, probs.astype(jnp.bfloat16), 1, 0)
            for slot in range(NEAR):
                columns = slice(slot * PATCH_NODES, (slot + 1) * PATCH_NODES)
                sums_ref[ids[slot], rows, :] += back_key[:, columns]
                sums_ref[ids[slot], value_rows, :] += back_value[:, columns]


def local_call(kernel, out_shape, flops, *operands):
    specs = [pl.BlockSpec(memory_space=pltpu.SMEM)] + [whole()] * (len(operands) - 1)
    return pl.pallas_call(
        kernel,
        out_shape=out_shape,
        in_specs=specs,
        out_specs=jax.tree.map(lambda leaf: whole(), out_shape),
        compiler_params=pltpu.CompilerParams(vmem_limit_bytes=VMEM_LIMIT),
        cost_estimate=pl.CostEstimate(flops=flops, bytes_accessed=8000000, transcendentals=3000000),
    )(*operands)


def inside(cell, count):
    return (cell >= 0) & (cell < count)


def greet(me, count):
    barrier = pltpu.get_barrier_semaphore()
    for step in OFFSETS:

        @pl.when(inside(me + step, count))
        def _():
            pl.semaphore_signal(barrier, inc=1, device_id={"cells": me + step}, device_id_type=MESH)

    pl.semaphore_wait(barrier, jnp.minimum(me, 2) + jnp.minimum(count - 1 - me, 2))


def spread_kernel(count, own_ref, window_ref, send_sem, recv_sem, own_sem):
    me = lax.axis_index("cells")
    own_copy = pltpu.make_async_copy(own_ref, window_ref.at[2], own_sem)
    own_copy.start()
    greet(me, count)
    copies = []
    for place, step in enumerate(OFFSETS):
        copy = pltpu.make_async_remote_copy(
            src_ref=own_ref,
            dst_ref=window_ref.at[2 - step],
            send_sem=send_sem.at[place],
            recv_sem=recv_sem.at[place],
            device_id={"cells": me + step},
            device_id_type=MESH,
        )
        copies.append(copy)
        pl.when(inside(me + step, count))(copy.start)
    own_copy.wait()
    for step, copy in zip(OFFSETS, copies):
        pl.when(inside(me + step, count))(copy.wait_send)
        pl.when(inside(me - step, count))(copy.wait_recv)


def spread(own):
    count = lax.axis_size("cells")
    return pl.pallas_call(
        functools.partial(spread_kernel, count),
        out_shape=jax.ShapeDtypeStruct((5,) + own.shape, own.dtype),
        in_specs=[whole()],
        out_specs=whole(),
        scratch_shapes=[
            pltpu.SemaphoreType.DMA((4,)),
            pltpu.SemaphoreType.DMA((4,)),
            pltpu.SemaphoreType.DMA,
        ],
        compiler_params=pltpu.CompilerParams(
            collective_id=0, has_side_effects=True, vmem_limit_bytes=VMEM_LIMIT
        ),
    )(own)


def collect_kernel(count, sums_ref, own_ref, outgoing, incoming, send_sem, recv_sem):
    me = lax.axis_index("cells")
    for place, step in enumerate(OFFSETS):
        outgoing[place] = sums_ref[2 + step].astype(jnp.bfloat16)
    greet(me, count)
    copies = []
    for place, step in enumerate(OFFSETS):
        copy = pltpu.make_async_remote_copy(
            src_ref=outgoing.at[place],
            dst_ref=incoming.at[place],
            send_sem=send_sem.at[place],
            recv_sem=recv_sem.at[place],
            device_id={"cells": me + step},
            device_id_type=MESH,
        )
        copies.append(copy)
        pl.when(inside(me + step, count))(copy.start)
    own_ref[...] = sums_ref[2]
    for place, (step, copy) in enumerate(zip(OFFSETS, copies)):

        @pl.when(inside(me - step, count))
        def _():
            copy.wait_recv()
            own_ref[...] += incoming[place].astype(jnp.float32)

    for step, copy in zip(OFFSETS, copies):
        pl.when(inside(me + step, count))(copy.wait_send)


def collect(sums):
    count = lax.axis_size("cells")
    slots = (4,) + sums.shape[1:]
    return pl.pallas_call(
        functools.partial(collect_kernel, count),
        out_shape=jax.ShapeDtypeStruct(sums.shape[1:], jnp.float32),
        in_specs=[whole()],
        out_specs=whole(),
        scratch_shapes=[
            pltpu.VMEM(slots, jnp.bfloat16),
            pltpu.VMEM(slots, jnp.bfloat16),
            pltpu.SemaphoreType.DMA((4,)),
            pltpu.SemaphoreType.DMA((4,)),
        ],
        compiler_params=pltpu.CompilerParams(
            collective_id=1, has_side_effects=True, vmem_limit_bytes=VMEM_LIMIT
        ),
    )(sums)


def reversed_bits(number, bits):
    return sum(((number >> bit) & 1) << (bits - 1 - bit) for bit in range(bits))


def halving_kernel(count, factor, term_ref, total_ref, first, later, send_sem, recv_sem):
    me = lax.axis_index("cells")
    bits = count.bit_length() - 1
    sides = [lax.rem(lax.div(me, 2**bit), 2) for bit in range(bits)]
    partners = [me + (1 - 2 * sides[bit]) * 2**bit for bit in range(bits)]
    barrier = pltpu.get_barrier_semaphore()
    for partner in partners:
        pl.semaphore_signal(barrier, inc=1, device_id={"cells": partner}, device_id_type=MESH)
    rows = total_ref.shape[0]
    for block in range(count):
        first[reversed_bits(block, bits)] = term_ref[block * rows : (block + 1) * rows, :].astype(
            jnp.bfloat16
        )
    pl.semaphore_wait(barrier, bits)
    copies = []
    source, base, start = first, 0, 0
    for bit in range(bits):
        half = count >> (bit + 1)
        copy = pltpu.make_async_remote_copy(
            src_ref=source.at[pl.ds(base + (1 - sides[bit]) * half, half)],
            dst_ref=later.at[pl.ds(start, half)],
            send_sem=send_sem.at[bit],
            recv_sem=recv_sem.at[bit],
            device_id={"cells": partners[bit]},
            device_id_type=MESH,
        )
        copy.start()
        copies.append(copy)
        copy.wait_recv()
        for block in range(half):
            mine = source[base + sides[bit] * half + block].astype(jnp.float32)
            added = mine + later[start + block].astype(jnp.float32)
            if bit == bits - 1:
                total_ref[...] = added * factor
            else:
                later[start + block] = added.astype(jnp.bfloat16)
        source, base, start = later, start, start + half
    for copy in copies:
        copy.wait_send()


def halving_scatter(term, factor):
    count = lax.axis_size("cells")
    bits = count.bit_length() - 1
    rows, columns = term.shape[0] // count, term.shape[1]
    return pl.pallas_call(
        functools.partial(halving_kernel, count, factor),
        out_shape=jax.ShapeDtypeStruct((rows, columns), jnp.float32),
        in_specs=[whole()],
        out_specs=whole(),
        scratch_shapes=[
            pltpu.VMEM((count, rows, columns), jnp.bfloat16),
            pltpu.VMEM((count, rows, columns), jnp.bfloat16),
            pltpu.SemaphoreType.DMA((bits,)),
            pltpu.SemaphoreType.DMA((bits,)),
        ],
        compiler_params=pltpu.CompilerParams(
            collective_id=2, has_side_effects=True, vmem_limit_bytes=VMEM_LIMIT
        ),
    )(term)


def per_device(
    features,
    cotangent,
    inner_weight,
    outer_weight,
    upward_weight,
    downward_weight,
    node_mask,
    neighbours,
):
    count = features.shape[0]
    patches = count // PATCH_NODES
    cells = lax.axis_size("cells")
    factor = (cells * count) ** (-0.5)
    position = lax.axis_index("cells")
    inputs = features.astype(jnp.float32)
    normed = rms_rows(inputs).astype(jnp.bfloat16)
    projected = jnp.dot(normed, inner_weight, preferred_element_type=jnp.float32)
    raw_queries = projected[:, :D]
    raw_keys = projected[:, D : 2 * D]
    queries = head_norm(raw_queries).astype(jnp.bfloat16)
    keys = head_norm(raw_keys).astype(jnp.bfloat16)
    values = projected[:, 2 * D :].astype(jnp.bfloat16)
    own = jnp.concatenate(
        [
            head_major(keys),
            head_major(values),
            jnp.broadcast_to(
                node_mask.astype(jnp.bfloat16)[:, None, :], (patches, 16, PATCH_NODES)
            ),
        ],
        axis=1,
    )
    window = spread(own).reshape(5 * patches, WINDOW_ROWS, PATCH_NODES)
    local_index = neighbours - (position - 2) * patches
    query_tiles = head_major(queries)
    products = 2 * patches * NEAR * PATCH_NODES * PATCH_NODES * D
    attended = row_major(
        local_call(
            forward_kernel,
            jax.ShapeDtypeStruct((patches, D, PATCH_NODES), jnp.bfloat16),
            2 * products,
            local_index,
            query_tiles,
            window,
        )
    )
    residual = (
        inputs + jnp.dot(attended, outer_weight, preferred_element_type=jnp.float32)
    ).astype(jnp.bfloat16)
    middle = residual.astype(jnp.float32)
    second = rms_rows(middle).astype(jnp.bfloat16)
    before = jnp.dot(second, upward_weight, preferred_element_type=jnp.float32)
    hidden = jax.nn.gelu(before).astype(jnp.bfloat16)
    back_hidden = jnp.dot(cotangent, downward_weight.T, preferred_element_type=jnp.float32)
    unused, gelu_back = jax.vjp(jax.nn.gelu, before)
    back_before = gelu_back(back_hidden)[0].astype(jnp.bfloat16)
    term_down = jnp.dot(hidden.T, cotangent, preferred_element_type=jnp.float32)
    term_up = jnp.dot(second.T, back_before, preferred_element_type=jnp.float32)
    back_second = jnp.dot(back_before, upward_weight.T, preferred_element_type=jnp.float32)
    unused, middle_back = jax.vjp(rms_rows, middle)
    back_residual = (cotangent.astype(jnp.float32) + middle_back(back_second)[0]).astype(
        jnp.bfloat16
    )
    back_attended = jnp.dot(
        back_residual, outer_weight.T, preferred_element_type=jnp.float32
    ).astype(jnp.bfloat16)
    term_outer = jnp.dot(attended.T, back_residual, preferred_element_type=jnp.float32)
    early = jnp.concatenate(
        [
            term_outer.reshape(cells, -1, D),
            term_up.reshape(cells, D // cells, -1, D).transpose(0, 2, 1, 3).reshape(cells, -1, D),
            term_down.reshape(cells, -1, D),
        ],
        axis=1,
    )
    summed = lax.psum_scatter(early, "cells", scatter_dimension=0, tiled=False) * factor
    back_query_tiles, sums = local_call(
        backward_kernel,
        (
            jax.ShapeDtypeStruct((patches, D, PATCH_NODES), jnp.float32),
            jax.ShapeDtypeStruct((5 * patches, 2 * D, PATCH_NODES), jnp.float32),
        ),
        5 * products,
        local_index,
        query_tiles,
        head_major(back_attended),
        window,
    )
    back_queries = row_major(back_query_tiles)
    collected = collect(sums.reshape(5, patches, 2 * D, PATCH_NODES))
    own_keys = row_major(collected[:, :D])
    own_values = row_major(collected[:, D:])
    unused, query_back = jax.vjp(head_norm, raw_queries)
    unused, key_back = jax.vjp(head_norm, raw_keys)
    back_projected = jnp.concatenate(
        [query_back(back_queries)[0], key_back(own_keys)[0], own_values],
        axis=-1,
    ).astype(jnp.bfloat16)
    term_inner = jnp.dot(normed.T, back_projected, preferred_element_type=jnp.float32)
    back_normed = jnp.dot(back_projected, inner_weight.T, preferred_element_type=jnp.float32)
    unused, input_back = jax.vjp(rms_rows, inputs)
    back_features = (back_residual.astype(jnp.float32) + input_back(back_normed)[0]).astype(
        jnp.bfloat16
    )
    rows = D // cells
    outer_rows, up_rows = rows, rows * (term_up.shape[1] // D)
    summed_up = summed[outer_rows : outer_rows + up_rows].reshape(-1, rows, D)
    return (
        back_features,
        halving_scatter(term_inner, factor),
        summed[:outer_rows],
        summed_up.transpose(1, 0, 2).reshape(rows, -1),
        summed[outer_rows + up_rows :],
    )


def solution(mesh):
    placed = (
        P(("groups", "cells"), None),
        P(("groups", "cells"), None),
        P(),
        P(),
        P(),
        P(),
        P(("groups", "cells"), None),
        P(("groups", "cells"), None),
    )
    return jax.shard_map(
        per_device,
        mesh=mesh,
        in_specs=placed,
        out_specs=(
            P(("groups", "cells"), None),
            P(("groups", "cells"), None),
            P(("groups", "cells"), None),
            P(("groups", "cells"), None),
            P(("groups", "cells"), None),
        ),
        check_vma=False,
    )
```

time: 453 us -> 240 us (0.53)
  waiting for transfers between devices: 200 us -> 0.02 us
  Pallas kernels: 0 us -> 140 us
  starting transfers between devices: 74.9 us -> 0.04 us
  matrix products: 65 us -> 16.4 us
  local copies, waits for them, and re-layouts: 68.1 us -> 53.3 us
  other arithmetic: 28.7 us -> 14.8 us
    pallas_call x0 -> x5, Pallas kernels: none -> 140 us  [the longest x1 46.3 us: collect(): pl.pallas_call(functools.partial(collect_kernel, count), out_shape=jax.Sh...]
    reduce_scatter x2 -> x0, waiting for transfers between devices: 129 us -> none  [the longest x1 64.6 us: per_device(): lax.psum_scatter(term_down, 'cells', scatter_dimension=0, tiled=True)]
    ppermute x20 -> x0, starting transfers between devices: 74.7 us -> none  [shifted(): lax.ppermute(value, axis, [(source, source + steps) for source in range(i...]
    unnamed x6 -> x2, waiting for transfers between devices: 56.4 us -> 0.02 us
    dot_general x8 -> x0, matrix products: 44.4 us -> none  [the longest x1 12.8 us: backward_block(): jnp.einsum('bhdi,bshdp->bhisp', back_block, near_values, preferred_elemen...]
    ppermute x20 -> x0, waiting for transfers between devices: 14.4 us -> none  [shifted(): lax.ppermute(value, axis, [(source, source + steps) for source in range(i...]
    reshape x10 -> x6, local copies, waits for them, and re-layouts: 18.5 us -> 6.02 us  [the longest x1 3.53 us: per_device(): term_up.reshape(cells, D // cells, -1, D).transpose(0, 2, 1, 3)]
    convert_element_type x4 -> x2, other arithmetic: 10.7 us -> 2.8 us  [the longest x1 2.11 us: per_device(): keys = head_norm(raw_keys).astype(jnp.bfloat16)]
  transfers between devices with their start and end apart: 24 -> 1, of which waited for: 7 -> 0; matrix products, arithmetic and copies ran while one was open for 21% -> 10% of each run, Pallas kernels for 0% -> 41%
where the time goes in v1:
time: 240 us; the launch traced here: 239 us
  Pallas kernels  140 us (58%)
  local copies, waits for them, and re-layouts  53.3 us (22%)
  matrix products  16.4 us (7%)
  other arithmetic  14.8 us (6%)
  between operations  14.5 us (6%)
    pallas_call x1, Pallas kernels, collect(): pl.pallas_call(functools.partial(collect_kernel, count), out_shape=jax.Sh...  46.3 us
    pallas_call x1, Pallas kernels, spread(): pl.pallas_call(functools.partial(spread_kernel, count), out_shape=jax.Sha...  36.5 us
    pallas_call x1, Pallas kernels, halving_scatter(): pl.pallas_call(functools.partial(halving_kernel, count, factor), out_shap...  35.5 us
    pallas_call x2, Pallas kernels, local_call(): pl.pallas_call(kernel, out_shape=out_shape, in_specs=specs, out_specs=jax...  21.7 us
    unnamed x64, local copies, waits for them, and re-layouts  12.6 us
    transpose x8, local copies, waits for them, and re-layouts, row_major(): return tiles.transpose(0, 2, 1).reshape(tiles.shape[0] * PATCH_NODES, D)  6.29 us
    broadcast_in_dim x4, local copies, waits for them, and re-layouts, head_norm(): jnp.mean(split * split, axis=-1, keepdims=True) + epsilon  6.04 us
    mul x4, local copies, waits for them, and re-layouts, head_norm(): split * lax.rsqrt(jnp.mean(split * split, axis=-1, keepdims=True) + epsilon)  5.99 us
  transfers between devices with their start and end apart: 1, of which 0 were waited for; matrix products, arithmetic and copies ran while one was open for 10% of the time, Pallas kernels for 41%

profile of v1, /device:TPU:0, one launch (start us, length us, event | category | flops | bytes accessed | tf_op | source)
XLA Modules:
  0.0 239.0 jit_solution(1485304043696443182)
XLA Ops:
  7.2 1.3 copy.70
  8.6 1.8 fusion.29
  10.5 1.2 fusion.43
  11.7 0.7 slice.61
  12.5 2.1 copy.71
  14.6 1.1 multiply_reduce_fusion.5
  15.7 0.9 mul.220
  16.6 2.1 copy.72
  18.7 2.1 copy.74
  20.9 1.1 multiply_reduce_fusion.4
  22.0 0.9 mul.224
  22.9 2.1 copy.75
  25.0 2.1 multiply_convert_fusion.3
  27.4 1.2 copy.77
  28.5 0.7 convert_element_type.52
  29.3 36.5 %shard_map.119 = bf16[5,3,784,128]{3,2,1,0:T(8,128)(2,1)S(1)} custom-call(bf16[3,784,128]{2,1,0:T(8,128)(2,1)S(1)} %pad_maximum_fusion.2.own_ref), custom_call_target="tpu_custom_call" | custom-call | tf_op jit(solution)/shard_map/pallas_call | solution.py:168
  65.8 1.6 copy-done.1
  67.7 1.8 copy-done.2
  69.5 6.7 %shard_map.120 = bf16[3,384,128]{2,1,0:T(8,128)(2,1)S(1)} custom-call(s32[3,8]{1,0:T(4,128)S(1)} %broadcast_subtract_fusion.index_ref, bf16[3,384,128]{2,1,0:T(8,128)(2,1)S(1)} %bitcast.74, bf16[15,784,128]{2,1,0:T(8,128)(2,1)S(1)} %bitcast.70), custom_call_target="tpu_custom_call" | custom-call | flops 603979776 | bytes 8000000 | tf_op jit(solution)/shard_map/pallas_call | solution.py:118
  76.3 0.3 copy.78
  76.5 0.4 multiply_reduce_fusion.3
  77.0 2.1 fusion.44
  79.1 3.5 %fusion.6 = (bf16[384,1536]{1,0:T(8,128)(2,1)S(1)}, f32[384,1536]{1,0:T(8,128)}) fusion(f32[384,1536]{1,0:T(8,128)S(1)} %fusion.44, bf16[384,1536]{1,0:T(8,128)(2,1)S(1)} %copy-done, f32[384,384]{0,1:T(8,128)S(1)} %get-tuple-element.38, f32[384]{0:T(512)S(1)} %fusion.36), kind=kOutput, calls=%fused_computation.9 | convolution fusion | flops 465076224 | bytes 7669248 | tf_op jit(solution)/shard_map/dot_general | solution.py:351
  82.6 2.2 fusion.31
  84.8 1.4 multiply_reduce_fusion.2
  86.2 1.2 copy.69
  87.3 3.5 %reshape.153 = f32[16,24,4,384]{3,2,1,0:T(4,128)} reshape(f32[384,1536]{1,0:T(8,128)} %fusion.31) | data formatting | bytes 4718592 | tf_op jit(solution)/shard_map/reshape | solution.py:370
  90.9 3.3 %copy.91 = f32[16,4,24,384]{3,2,1,0:T(8,128)} copy(f32[16,4,24,384]{3,1,2,0:T(4,128)} %bitcast.78) | data formatting | bytes 4718592 | tf_op jit(solution)/shard_map/transpose | solution.py:370
  94.1 0.6 multiply_multiply_fusion.5
  94.7 0.9 copy.89
  95.6 2.9 %fusion.9 = f32[1536,384]{1,0:T(8,128)S(1)} fusion(bf16[384,384]{1,0:T(8,128)(2,1)} %param.9, f32[384,1536]{1,0:T(8,128)} %get-tuple-element.40), kind=kOutput, calls=%fused_computation.15 | convolution fusion | flops 458293248 | bytes 5013504 | tf_op jit(solution)/shard_map/dot_general | solution.py:356
  98.7 0.4 fusion.26
  99.1 1.2 copy-done.5
  100.3 2.7 %pad_maximum_fusion = f32[16,216,384]{2,1,0:T(8,128)} fusion(f32[16,96,384]{2,1,0:T(8,128)S(1)} %bitcast.90, f32[16,96,384]{2,1,0:T(8,128)S(1)} %bitcast.79, f32[16,24,384]{2,1,0:T(8,128)S(1)} %fusion.26), kind=kLoop, calls=%fused_computation | loop fusion | flops 2654208 | bytes 10616832 | tf_op jit(solution)/shard_map/concatenate | solution.py:367
  103.0 0.9 copy-done.13
  103.9 0.4 convolution_convert_fusion
  104.5 1.9 copy-done.3
  106.4 15.0 %shard_map.121 = (f32[3,384,128]{2,1,0:T(8,128)S(1)}, f32[15,768,128]{2,1,0:T(8,128)S(1)}) custom-call(s32[3,8]{1,0:T(4,128)S(1)} %broadcast_subtract_fusion.index_ref, bf16[3,384,128]{2,1,0:T(8,128)(2,1)S(1)} %bitcast.75, bf16[3,384,128]{2,1,0:T(8,128)(2,1)S(1)} %bitcast.76, bf16[15,784,128]{2,1,0:T(8,128)(2,1)S(1)} %bitcast.71), custom_call_target="tpu_custom_call" | custom-call | flops 1509949440 | bytes 8000000 | tf_op jit(solution)/shard_map/pallas_call | solution.py:118
  121.4 46.3 %shard_map.122 = f32[3,768,128]{2,1,0:T(8,128)S(1)} custom-call(f32[5,3,768,128]{3,2,1,0:T(8,128)S(1)} %bitcast.69), custom_call_target="tpu_custom_call" | custom-call | tf_op jit(solution)/shard_map/pallas_call | solution.py:216
  167.8 0.8 copy-done.7
  168.6 1.3 copy.86
  169.9 2.1 copy.84
  172.0 1.3 copy.82
  173.3 1.0 copy.80
  174.4 2.3 reshape_reshape.13
  176.7 1.4 multiply_reduce_fusion
  178.1 0.9 broadcast_in_dim.34
  179.0 2.1 copy.87
  181.1 2.3 reshape_reshape.11
  183.4 1.2 multiply_reduce_fusion.1
  184.7 0.9 broadcast_in_dim.32
  185.5 2.1 copy.83
  187.7 0.2 copy.88
  187.9 2.4 %fusion.16 = (bf16[384,384]{1,0:T(8,128)(2,1)S(1)}, bf16[384,384]{1,0:T(8,128)(2,1)S(1)}) fusion(f32[384,384]{1,0:T(8,128)S(1)} %copy-done.8, f32[3,128,384]{2,1,0:T(8,128)} %copy.80, f32[384,384]{1,0:T(8,128)} %copy.83, f32[384,1152]{1,0:T(8,128)} %copy-done.4, f32[384,384]{1,0:T(8,128)} %copy.87, f32[384,384]{1,0:T(8,128)} %copy.75, f32[3,128,384]{2,1,0:T(8,128)} %copy.84), kind=kLoop, calls=%fused_computation.32 | loop fusion | flops 1474560 | bytes 5308416 | tf_op jit(solution)/shard_map/convert
  190.4 0.6 fusion.23.term_ref
  191.0 35.5 %shard_map.123 = f32[24,1152]{1,0:T(8,128)S(1)} custom-call(f32[384,1152]{1,0:T(8,128)S(1)} %fusion.23.term_ref), custom_call_target="tpu_custom_call" | custom-call | tf_op jit(solution)/shard_map/pallas_call | solution.py:282
  226.5 0.7 fusion.22
  227.3 0.2 copy-done.10
  227.7 0.9 copy.93
  228.6 1.0 broadcast_multiply_fusion
  229.6 0.7 slice_bitcast_fusion.1
  230.2 0.6 slice_bitcast_fusion.2
  230.9 0.7 copy.96
  231.5 0.6 copy.98
  (74 shorter events, 1.4 us)
Async XLA Ops:
  7.2 71.9 %copy-start = (bf16[384,1536]{1,0:T(8,128)(2,1)S(1)}, bf16[384,1536]{1,0:T(8,128)(2,1)}, u32[]{:S(2)}) copy-start(bf16[384,1536]{1,0:T(8,128)(2,1)} %param.12) | copy-start | bytes 3538948
  7.2 221.4 %reduce-scatter.4.cloned.1.call-start = ((), (), s32[]{:S(2)}) async-start(), calls=%async_computation.1 | async-start | bytes 5640192
  8.6 3.1 %copy-start.23 = (f32[384]{0:T(512)}, f32[384]{0:T(512)S(1)}, u32[]{:S(2)}) copy-start(f32[384]{0:T(512)S(1)} %fusion.20) | copy-start | bytes 4612
  8.6 3.1 %copy-start.21 = (f32[384]{0:T(512)}, f32[384]{0:T(512)S(1)}, u32[]{:S(2)}) copy-start(f32[384]{0:T(512)S(1)} %fusion.35) | copy-start | bytes 4612
  10.5 14.6 %copy-start.4 = (f32[384,1152]{1,0:T(8,128)}, f32[384,1152]{1,0:T(8,128)S(1)}, u32[]{:S(2)}) copy-start(f32[384,1152]{1,0:T(8,128)S(1)} %fusion.29) | copy-start | bytes 5308420
  22.0 0.9 copy-start.17
  29.2 38.2 %copy-start.11 = (bf16[384,384]{1,0:T(8,128)(2,1)S(1)}, bf16[384,384]{1,0:T(8,128)(2,1)}, u32[]{:S(2)}) copy-start(bf16[384,384]{1,0:T(8,128)(2,1)} %get-tuple-element.32) | copy-start | bytes 884740
  29.3 38.4 %copy-start.29 = (s32[3,8]{1,0:T(4,128)S(1)}, s32[3,8]{1,0:T(4,128)}, u32[]{:S(2)}) copy-start(s32[3,8]{1,0:T(4,128)} %param.15) | copy-start | bytes 292
  65.8 1.6 copy-start.1
  67.7 1.9 copy-start.2
  69.5 7.0 %copy-start.12 = (bf16[384,384]{1,0:T(8,128)(2,1)S(1)}, bf16[384,384]{1,0:T(8,128)(2,1)}, u32[]{:S(2)}) copy-start(bf16[384,384]{1,0:T(8,128)(2,1)} %param.11) | copy-start | bytes 884740
  69.5 7.4 %copy-start.15 = (bf16[384,384]{1,0:T(8,128)(2,1)S(1)}, bf16[384,384]{1,0:T(8,128)(2,1)}, u32[]{:S(2)}) copy-start(bf16[384,384]{1,0:T(8,128)(2,1)} %param.9) | copy-start | bytes 884740
  76.9 5.6 %copy-start.25 = (f32[384]{0:T(512)}, f32[384]{0:T(512)S(1)}, u32[]{:S(2)}) copy-start(f32[384]{0:T(512)S(1)} %get-tuple-element.37) | copy-start | bytes 4612
  77.0 5.6 %copy-start.19 = (f32[384]{0:T(512)}, f32[384]{0:T(512)S(1)}, u32[]{:S(2)}) copy-start(f32[384]{0:T(512)S(1)} %fusion.36) | copy-start | bytes 4612
  90.9 3.3 %copy-start.26 = (f32[384]{0:T(512)S(1)}, f32[384]{0:T(512)}, u32[]{:S(2)}) copy-start(f32[384]{0:T(512)} %copy-done.25) | copy-start | bytes 4612
  90.9 3.3 %copy-start.28 = (f32[384]{0:T(512)S(1)}, f32[384]{0:T(512)}, u32[]{:S(2)}) copy-start(f32[384]{0:T(512)} %get-tuple-element.41) | copy-start | bytes 4612
  95.6 2.9 %copy-start.20 = (f32[384]{0:T(512)S(1)}, f32[384]{0:T(512)}, u32[]{:S(2)}) copy-start(f32[384]{0:T(512)} %copy-done.19) | copy-start | bytes 4612
  95.6 2.9 %copy-start.27 = (f32[384]{0:T(512)S(1)}, f32[384]{0:T(512)}, u32[]{:S(2)}) copy-start(f32[384]{0:T(512)} %multiply_multiply_fusion.5) | copy-start | bytes 4612
  95.6 3.1 %copy-start.14 = (bf16[384,384]{1,0:T(8,128)(2,1)S(1)}, bf16[384,384]{1,0:T(8,128)(2,1)}, u32[]{:S(2)}) copy-start(bf16[384,384]{1,0:T(8,128)(2,1)} %copy.89) | copy-start | bytes 884740
  98.5 1.8 copy-start.5
  98.7 4.3 %copy-start.9 = (bf16[384,384]{0,1:T(8,128)(2,1)}, bf16[384,384]{0,1:T(8,128)(2,1)S(1)}, u32[]{:S(2)}) copy-start(bf16[384,384]{0,1:T(8,128)(2,1)S(1)} %fusion.15) | copy-start | bytes 884740
  102.9 1.0 copy-start.13
  104.5 1.9 copy-start.3
  167.8 0.8 copy-start.7
  172.0 6.0 %copy-start.18 = (f32[384,8]{0,1:T(8,128)S(1)}, f32[384,8]{0,1:T(8,128)}, u32[]{:S(2)}) copy-start(f32[384,8]{0,1:T(8,128)} %copy-done.17) | copy-start | bytes 36868
  176.7 6.8 %copy-start.6 = (f32[384,384]{0,1:T(8,128)S(1)}, f32[384,384]{0,1:T(8,128)}, u32[]{:S(2)}) copy-start(f32[384,384]{0,1:T(8,128)} %copy.71) | copy-start | bytes 1769476
  184.6 3.3 %copy-start.8 = (f32[384,384]{1,0:T(8,128)S(1)}, f32[384,384]{1,0:T(8,128)}, u32[]{:S(2)}) copy-start(f32[384,384]{1,0:T(8,128)} %copy.72) | copy-start | bytes 1769476
  187.9 2.4 %copy-start.22 = (f32[384]{0:T(512)S(1)}, f32[384]{0:T(512)}, u32[]{:S(2)}) copy-start(f32[384]{0:T(512)} %copy-done.21) | copy-start | bytes 4612
  190.3 36.2 %copy-start.16 = (bf16[384,1152]{1,0:T(8,128)(2,1)S(1)}, bf16[384,1152]{1,0:T(8,128)(2,1)}, u32[]{:S(2)}) copy-start(bf16[384,1152]{1,0:T(8,128)(2,1)} %param.10) | copy-start | bytes 2654212
  226.5 0.7 copy-start.24
  226.5 1.0 copy-start.10
Sparse Core Ops, SparseCore 0:
  103.1 111.1 reduce-scatter.3
